TPU v7x, 128 devices: a whole 4x4x4 slice. The times are simulated.
128 devices in a mesh: group: 16 (over x_lo, z, core), inner: 8 (over y, x_hi).
Axes of the slice: x: 4 (x_hi: 2, x_lo: 2; x = x_hi * 2 + x_lo), y: 4, z: 4, core: 2. Of those that a mesh axis runs over, the one named last changes fastest.
Arguments:
- clips: bfloat16 [16384, 8, 1152], P(('group', 'inner')), may hold values from -6 to 6
- counts: int32 [16384], P(('group', 'inner')), may hold values from 1 to 8
- texts: bfloat16 [16384, 1152], P(('group', 'inner')), may hold values from -6 to 6
- log_scale: float32 [1], replicated, may hold values from 2 to 3
- bias: float32 [1], replicated, may hold values from -3 to -1
Outputs:
- clip_grad: float32 [16384, 8, 1152], P(('group', 'inner'))
- text_grad: float32 [16384, 1152], P(('group', 'inner'))
Inputs may be any that keep to these rules, and one draw needn't show every extreme that they name: `counts`: slots at and beyond a video's count are ignored.
All inputs are finite; a program needn't handle non-finite values.
Results may differ from a plain program's by a relative error of at most 0.0048.
Values may be sent and summed in bfloat16 or wider, within the bound.
A program may use at most 256 MiB of HBM per device.

v0:
```python
import jax
import jax.numpy as jnp
from jax import lax
from jax.sharding import PartitionSpec as P


def shifted(block, axis, distance):
    devices = range(lax.axis_size(axis))
    route = [((i - distance) % len(devices), i) for i in devices]
    return lax.ppermute(block, axis, route)


def unit_rows(values):
    norm = jnp.sqrt(jnp.sum(values * values, axis=1, keepdims=True) + 1e-06)
    return (values / norm, norm)


def on_device(clips, counts, texts, log_scale, bias):
    videos = clips.shape[0]
    slot_count = clips.shape[1]
    slot_ids = lax.broadcasted_iota(jnp.int32, (videos, slot_count), 1)
    used = (slot_ids < counts[:, None]).astype(jnp.float32)
    count_f = counts.astype(jnp.float32)
    pooled = jnp.sum(clips.astype(jnp.float32) * used[:, :, None], axis=1) / count_f[:, None]
    vid_unit, vid_norm = unit_rows(pooled)
    vid_half = vid_unit.astype(jnp.bfloat16)
    txt_unit, txt_norm = unit_rows(texts.astype(jnp.float32))
    txt_half = txt_unit.astype(jnp.bfloat16)
    scale = jnp.exp(log_scale[0])
    offset = bias[0]
    groups = lax.axis_size("group")
    inners = lax.axis_size("inner")
    group_id = lax.axis_index("group")
    inner_id = lax.axis_index("inner")
    device = group_id * inners + inner_id
    row_ids = lax.broadcasted_iota(jnp.int32, (videos, 1), 0) + device * videos

    def block_coef(left, right, left_ids, right_ids):
        logits = scale * jnp.dot(left, right.T, preferred_element_type=jnp.float32) + offset
        match = (right_ids == left_ids).astype(jnp.float32)
        return (jax.nn.sigmoid(logits) - match).astype(jnp.bfloat16)

    def pair_block(block, first_col):
        col_ids = lax.broadcasted_iota(jnp.int32, (1, block.shape[0]), 1) + first_col
        return block_coef(vid_half, block, row_ids, col_ids)

    def back_terms(coef):
        return scale * lax.dot_general(
            coef, vid_half, (((0,), (0,)), ((), ())), preferred_element_type=jnp.float32
        )

    block = lax.all_gather(txt_half, "inner", axis=0, tiled=True)
    width = block.shape[1]
    holder = jnp.zeros((block.shape[0], width), jnp.float32)
    vid_acc = jnp.zeros((videos, width), jnp.float32)

    def one_round(step, carry):
        current, terms, vid_sum = carry
        source = (group_id - step + groups) % groups
        coef = pair_block(current, source * inners * videos)
        vid_sum = vid_sum + scale * jnp.dot(coef, current, preferred_element_type=jnp.float32)
        terms = terms + back_terms(coef)
        current = shifted(current, "group", 1)
        terms = shifted(terms, "group", 1)
        return (current, terms, vid_sum)

    block, holder, vid_back = lax.fori_loop(0, groups, one_round, (block, holder, vid_acc))
    txt_back = lax.psum_scatter(holder, "inner", scatter_dimension=0, tiled=True)
    text_grad = (
        txt_back - txt_unit * jnp.sum(txt_unit * txt_back, axis=1, keepdims=True)
    ) / txt_norm
    pool_back = (
        vid_back - vid_unit * jnp.sum(vid_unit * vid_back, axis=1, keepdims=True)
    ) / vid_norm
    clip_grad = (pool_back / count_f[:, None])[:, None, :] * used[:, :, None]
    return (clip_grad, text_grad)


def solution(mesh):
    return jax.shard_map(
        on_device,
        mesh=mesh,
        in_specs=(
            P(("group", "inner"), None, None),
            P(("group", "inner")),
            P(("group", "inner"), None),
            P(),
            P(),
        ),
        out_specs=(P(("group", "inner"), None, None), P(("group", "inner"), None)),
        check_vma=False,
    )
```

profile of v0, /device:TPU:1, one launch (start us, length us, event | category | flops | bytes accessed | tf_op | source)
XLA Modules:
  0.0 1602.3 jit_solution(3765416872250765266)
XLA Ops:
  16.4 53.2 %all-gather.2.cloned.1.call-done = bf16[1024,1152]{1,0:T(8,128)(2,1)} async-done(((bf16[128,1152]{1,0:T(8,128)(2,1)}), bf16[1024,1152]{1,0:T(8,128)(2,1)}) %all-gather.2.cloned.1.call-update) | async-done | bytes 2359312 | tf_op jit(solution)/shard_map/all_gather | solution.py:52
  72.1 1403.5 %while.20 = (s32[]{:T(128)}, bf16[1024,1152]{1,0:T(8,128)(2,1)}, f32[1024,1152]{1,0:T(8,128)}, f32[128,1152]{1,0:T(8,128)S(1)}, f32[]{:T(128)}, /*index=5*/bf16[...) while((s32[]{:T(128)}, bf16[1024,1152]{1,0:T(8,128)(2,1)}, ...), condition=%wide.region_4.5_spmd.clone, body=%wide.region_3.4_spmd.clone.sunk | while | flops 909952128 | bytes 49751428 | solution.py:67
  75.3 5.3 fusion.37
  83.6 75.9 %collective-permute-done = bf16[1024,1152]{1,0:T(8,128)(2,1)} collective-permute-done((bf16[1024,1152]{1,0:T(8,128)(2,1)S(1)}, bf16[1024,1152]{1,0:T(8,128)(2,1)}, u32[]{:S(2)}, u32[]{:S(2)}) %collective-permute-start) | collective-permute-done | bytes 2359328 | tf_op jit(solution)/shard_map/while/body/eval_jaxpr/ppermute | solution.py:10
  162.7 5.3 fusion.37
  171.3 75.9 %collective-permute-done = bf16[1024,1152]{1,0:T(8,128)(2,1)} collective-permute-done((bf16[1024,1152]{1,0:T(8,128)(2,1)S(1)}, bf16[1024,1152]{1,0:T(8,128)(2,1)}, u32[]{:S(2)}, u32[]{:S(2)}) %collective-permute-start) | collective-permute-done | bytes 2359328 | tf_op jit(solution)/shard_map/while/body/eval_jaxpr/ppermute | solution.py:10
  250.5 5.3 fusion.37
  259.0 75.9 %collective-permute-done = bf16[1024,1152]{1,0:T(8,128)(2,1)} collective-permute-done((bf16[1024,1152]{1,0:T(8,128)(2,1)S(1)}, bf16[1024,1152]{1,0:T(8,128)(2,1)}, u32[]{:S(2)}, u32[]{:S(2)}) %collective-permute-start) | collective-permute-done | bytes 2359328 | tf_op jit(solution)/shard_map/while/body/eval_jaxpr/ppermute | solution.py:10
  338.2 5.3 fusion.37
  346.8 75.9 %collective-permute-done = bf16[1024,1152]{1,0:T(8,128)(2,1)} collective-permute-done((bf16[1024,1152]{1,0:T(8,128)(2,1)S(1)}, bf16[1024,1152]{1,0:T(8,128)(2,1)}, u32[]{:S(2)}, u32[]{:S(2)}) %collective-permute-start) | collective-permute-done | bytes 2359328 | tf_op jit(solution)/shard_map/while/body/eval_jaxpr/ppermute | solution.py:10
  425.9 5.3 fusion.37
  434.5 75.9 %collective-permute-done = bf16[1024,1152]{1,0:T(8,128)(2,1)} collective-permute-done((bf16[1024,1152]{1,0:T(8,128)(2,1)S(1)}, bf16[1024,1152]{1,0:T(8,128)(2,1)}, u32[]{:S(2)}, u32[]{:S(2)}) %collective-permute-start) | collective-permute-done | bytes 2359328 | tf_op jit(solution)/shard_map/while/body/eval_jaxpr/ppermute | solution.py:10
  522.3 75.9 %collective-permute-done = bf16[1024,1152]{1,0:T(8,128)(2,1)} collective-permute-done((bf16[1024,1152]{1,0:T(8,128)(2,1)S(1)}, bf16[1024,1152]{1,0:T(8,128)(2,1)}, u32[]{:S(2)}, u32[]{:S(2)}) %collective-permute-start) | collective-permute-done | bytes 2359328 | tf_op jit(solution)/shard_map/while/body/eval_jaxpr/ppermute | solution.py:10
  610.0 75.9 %collective-permute-done = bf16[1024,1152]{1,0:T(8,128)(2,1)} collective-permute-done((bf16[1024,1152]{1,0:T(8,128)(2,1)S(1)}, bf16[1024,1152]{1,0:T(8,128)(2,1)}, u32[]{:S(2)}, u32[]{:S(2)}) %collective-permute-start) | collective-permute-done | bytes 2359328 | tf_op jit(solution)/shard_map/while/body/eval_jaxpr/ppermute | solution.py:10
  697.7 75.9 %collective-permute-done = bf16[1024,1152]{1,0:T(8,128)(2,1)} collective-permute-done((bf16[1024,1152]{1,0:T(8,128)(2,1)S(1)}, bf16[1024,1152]{1,0:T(8,128)(2,1)}, u32[]{:S(2)}, u32[]{:S(2)}) %collective-permute-start) | collective-permute-done | bytes 2359328 | tf_op jit(solution)/shard_map/while/body/eval_jaxpr/ppermute | solution.py:10
  785.5 75.9 %collective-permute-done = bf16[1024,1152]{1,0:T(8,128)(2,1)} collective-permute-done((bf16[1024,1152]{1,0:T(8,128)(2,1)S(1)}, bf16[1024,1152]{1,0:T(8,128)(2,1)}, u32[]{:S(2)}, u32[]{:S(2)}) %collective-permute-start) | collective-permute-done | bytes 2359328 | tf_op jit(solution)/shard_map/while/body/eval_jaxpr/ppermute | solution.py:10
  873.2 75.9 %collective-permute-done = bf16[1024,1152]{1,0:T(8,128)(2,1)} collective-permute-done((bf16[1024,1152]{1,0:T(8,128)(2,1)S(1)}, bf16[1024,1152]{1,0:T(8,128)(2,1)}, u32[]{:S(2)}, u32[]{:S(2)}) %collective-permute-start) | collective-permute-done | bytes 2359328 | tf_op jit(solution)/shard_map/while/body/eval_jaxpr/ppermute | solution.py:10
  960.9 75.9 %collective-permute-done = bf16[1024,1152]{1,0:T(8,128)(2,1)} collective-permute-done((bf16[1024,1152]{1,0:T(8,128)(2,1)S(1)}, bf16[1024,1152]{1,0:T(8,128)(2,1)}, u32[]{:S(2)}, u32[]{:S(2)}) %collective-permute-start) | collective-permute-done | bytes 2359328 | tf_op jit(solution)/shard_map/while/body/eval_jaxpr/ppermute | solution.py:10
  1048.7 75.9 %collective-permute-done = bf16[1024,1152]{1,0:T(8,128)(2,1)} collective-permute-done((bf16[1024,1152]{1,0:T(8,128)(2,1)S(1)}, bf16[1024,1152]{1,0:T(8,128)(2,1)}, u32[]{:S(2)}, u32[]{:S(2)}) %collective-permute-start) | collective-permute-done | bytes 2359328 | tf_op jit(solution)/shard_map/while/body/eval_jaxpr/ppermute | solution.py:10
  1136.4 75.9 %collective-permute-done = bf16[1024,1152]{1,0:T(8,128)(2,1)} collective-permute-done((bf16[1024,1152]{1,0:T(8,128)(2,1)S(1)}, bf16[1024,1152]{1,0:T(8,128)(2,1)}, u32[]{:S(2)}, u32[]{:S(2)}) %collective-permute-start) | collective-permute-done | bytes 2359328 | tf_op jit(solution)/shard_map/while/body/eval_jaxpr/ppermute | solution.py:10
  1224.2 75.9 %collective-permute-done = bf16[1024,1152]{1,0:T(8,128)(2,1)} collective-permute-done((bf16[1024,1152]{1,0:T(8,128)(2,1)S(1)}, bf16[1024,1152]{1,0:T(8,128)(2,1)}, u32[]{:S(2)}, u32[]{:S(2)}) %collective-permute-start) | collective-permute-done | bytes 2359328 | tf_op jit(solution)/shard_map/while/body/eval_jaxpr/ppermute | solution.py:10
  1311.9 75.9 %collective-permute-done = bf16[1024,1152]{1,0:T(8,128)(2,1)} collective-permute-done((bf16[1024,1152]{1,0:T(8,128)(2,1)S(1)}, bf16[1024,1152]{1,0:T(8,128)(2,1)}, u32[]{:S(2)}, u32[]{:S(2)}) %collective-permute-start) | collective-permute-done | bytes 2359328 | tf_op jit(solution)/shard_map/while/body/eval_jaxpr/ppermute | solution.py:10
  1399.6 75.9 %collective-permute-done = bf16[1024,1152]{1,0:T(8,128)(2,1)} collective-permute-done((bf16[1024,1152]{1,0:T(8,128)(2,1)S(1)}, bf16[1024,1152]{1,0:T(8,128)(2,1)}, u32[]{:S(2)}, u32[]{:S(2)}) %collective-permute-start) | collective-permute-done | bytes 2359328 | tf_op jit(solution)/shard_map/while/body/eval_jaxpr/ppermute | solution.py:10
  1479.6 112.5 %reduce-scatter.2.cloned.1.call-done = f32[128,1152]{1,0:T(8,128)} async-done(((f32[1024,1152]{1,0:T(8,128)}), f32[128,1152]{1,0:T(8,128)}) %reduce-scatter.2.cloned.1.call-update) | async-done | bytes 589840 | tf_op jit(solution)/shard_map/reduce_scatter | solution.py:68
  (171 shorter events, 180.2 us)
Async XLA Ops:
  10.2 1581.9 %reduce-scatter.2.cloned.1.call-start = ((), (), s32[]{:S(2)}) async-start(), calls=%async_computation.2 | async-start | bytes 5308416 | tf_op jit(solution)/shard_map/reduce_scatter | solution.py:68
  80.7 78.8 %collective-permute-start.1 = (f32[1024,1152]{1,0:T(8,128)}, f32[1024,1152]{1,0:T(8,128)}, u32[]{:S(2)}, u32[]{:S(2)}) collective-permute-start(f32[1024,1152]{1,0:T(8,128)} %fusion.37), channel_id=1, source_target_pairs={{120,0},{0,8},{8,16},{16,24},{24,32},{32,40},{40,48},{48,56},{56,6... | collective-permute-start | bytes 14155784 | tf_op jit(solution)/shard_map/while/body/eval_jaxpr/ppermute | solution.py:10
  168.1 79.2 %collective-permute-start.1 = (f32[1024,1152]{1,0:T(8,128)}, f32[1024,1152]{1,0:T(8,128)}, u32[]{:S(2)}, u32[]{:S(2)}) collective-permute-start(f32[1024,1152]{1,0:T(8,128)} %fusion.37), channel_id=1, source_target_pairs={{120,0},{0,8},{8,16},{16,24},{24,32},{32,40},{40,48},{48,56},{56,6... | collective-permute-start | bytes 14155784 | tf_op jit(solution)/shard_map/while/body/eval_jaxpr/ppermute | solution.py:10
  170.7 76.6 %collective-permute-start = (bf16[1024,1152]{1,0:T(8,128)(2,1)S(1)}, bf16[1024,1152]{1,0:T(8,128)(2,1)}, u32[]{:S(2)}, u32[]{:S(2)}) collective-permute-start(bf16[1024,1152]{1,0:T(8,128)(2,1)S(1)} %copy.12), channel_id=1, source_target_pairs={{120,0},{0,8},{8,16},{16,24},{24,32},{32,40},{40,48},{48,56},{56,6... | collective-permute-start | bytes 7077896 | tf_op jit(solution)/shard_map/while/body/eval_jaxpr/ppermute | solution.py:10
  255.8 79.2 %collective-permute-start.1 = (f32[1024,1152]{1,0:T(8,128)}, f32[1024,1152]{1,0:T(8,128)}, u32[]{:S(2)}, u32[]{:S(2)}) collective-permute-start(f32[1024,1152]{1,0:T(8,128)} %fusion.37), channel_id=1, source_target_pairs={{120,0},{0,8},{8,16},{16,24},{24,32},{32,40},{40,48},{48,56},{56,6... | collective-permute-start | bytes 14155784 | tf_op jit(solution)/shard_map/while/body/eval_jaxpr/ppermute | solution.py:10
  343.5 79.2 %collective-permute-start.1 = (f32[1024,1152]{1,0:T(8,128)}, f32[1024,1152]{1,0:T(8,128)}, u32[]{:S(2)}, u32[]{:S(2)}) collective-permute-start(f32[1024,1152]{1,0:T(8,128)} %fusion.37), channel_id=1, source_target_pairs={{120,0},{0,8},{8,16},{16,24},{24,32},{32,40},{40,48},{48,56},{56,6... | collective-permute-start | bytes 14155784 | tf_op jit(solution)/shard_map/while/body/eval_jaxpr/ppermute | solution.py:10
  431.3 79.2 %collective-permute-start.1 = (f32[1024,1152]{1,0:T(8,128)}, f32[1024,1152]{1,0:T(8,128)}, u32[]{:S(2)}, u32[]{:S(2)}) collective-permute-start(f32[1024,1152]{1,0:T(8,128)} %fusion.37), channel_id=1, source_target_pairs={{120,0},{0,8},{8,16},{16,24},{24,32},{32,40},{40,48},{48,56},{56,6... | collective-permute-start | bytes 14155784 | tf_op jit(solution)/shard_map/while/body/eval_jaxpr/ppermute | solution.py:10
  433.9 76.6 %collective-permute-start = (bf16[1024,1152]{1,0:T(8,128)(2,1)S(1)}, bf16[1024,1152]{1,0:T(8,128)(2,1)}, u32[]{:S(2)}, u32[]{:S(2)}) collective-permute-start(bf16[1024,1152]{1,0:T(8,128)(2,1)S(1)} %copy.12), channel_id=1, source_target_pairs={{120,0},{0,8},{8,16},{16,24},{24,32},{32,40},{40,48},{48,56},{56,6... | collective-permute-start | bytes 7077896 | tf_op jit(solution)/shard_map/while/body/eval_jaxpr/ppermute | solution.py:10
  519.0 79.2 %collective-permute-start.1 = (f32[1024,1152]{1,0:T(8,128)}, f32[1024,1152]{1,0:T(8,128)}, u32[]{:S(2)}, u32[]{:S(2)}) collective-permute-start(f32[1024,1152]{1,0:T(8,128)} %fusion.37), channel_id=1, source_target_pairs={{120,0},{0,8},{8,16},{16,24},{24,32},{32,40},{40,48},{48,56},{56,6... | collective-permute-start | bytes 14155784 | tf_op jit(solution)/shard_map/while/body/eval_jaxpr/ppermute | solution.py:10
  606.8 79.2 %collective-permute-start.1 = (f32[1024,1152]{1,0:T(8,128)}, f32[1024,1152]{1,0:T(8,128)}, u32[]{:S(2)}, u32[]{:S(2)}) collective-permute-start(f32[1024,1152]{1,0:T(8,128)} %fusion.37), channel_id=1, source_target_pairs={{120,0},{0,8},{8,16},{16,24},{24,32},{32,40},{40,48},{48,56},{56,6... | collective-permute-start | bytes 14155784 | tf_op jit(solution)/shard_map/while/body/eval_jaxpr/ppermute | solution.py:10
  609.3 76.6 %collective-permute-start = (bf16[1024,1152]{1,0:T(8,128)(2,1)S(1)}, bf16[1024,1152]{1,0:T(8,128)(2,1)}, u32[]{:S(2)}, u32[]{:S(2)}) collective-permute-start(bf16[1024,1152]{1,0:T(8,128)(2,1)S(1)} %copy.12), channel_id=1, source_target_pairs={{120,0},{0,8},{8,16},{16,24},{24,32},{32,40},{40,48},{48,56},{56,6... | collective-permute-start | bytes 7077896 | tf_op jit(solution)/shard_map/while/body/eval_jaxpr/ppermute | solution.py:10
  694.5 79.2 %collective-permute-start.1 = (f32[1024,1152]{1,0:T(8,128)}, f32[1024,1152]{1,0:T(8,128)}, u32[]{:S(2)}, u32[]{:S(2)}) collective-permute-start(f32[1024,1152]{1,0:T(8,128)} %fusion.37), channel_id=1, source_target_pairs={{120,0},{0,8},{8,16},{16,24},{24,32},{32,40},{40,48},{48,56},{56,6... | collective-permute-start | bytes 14155784 | tf_op jit(solution)/shard_map/while/body/eval_jaxpr/ppermute | solution.py:10
  697.1 76.6 %collective-permute-start = (bf16[1024,1152]{1,0:T(8,128)(2,1)S(1)}, bf16[1024,1152]{1,0:T(8,128)(2,1)}, u32[]{:S(2)}, u32[]{:S(2)}) collective-permute-start(bf16[1024,1152]{1,0:T(8,128)(2,1)S(1)} %copy.12), channel_id=1, source_target_pairs={{120,0},{0,8},{8,16},{16,24},{24,32},{32,40},{40,48},{48,56},{56,6... | collective-permute-start | bytes 7077896 | tf_op jit(solution)/shard_map/while/body/eval_jaxpr/ppermute | solution.py:10
  782.2 79.2 %collective-permute-start.1 = (f32[1024,1152]{1,0:T(8,128)}, f32[1024,1152]{1,0:T(8,128)}, u32[]{:S(2)}, u32[]{:S(2)}) collective-permute-start(f32[1024,1152]{1,0:T(8,128)} %fusion.37), channel_id=1, source_target_pairs={{120,0},{0,8},{8,16},{16,24},{24,32},{32,40},{40,48},{48,56},{56,6... | collective-permute-start | bytes 14155784 | tf_op jit(solution)/shard_map/while/body/eval_jaxpr/ppermute | solution.py:10
  870.0 79.2 %collective-permute-start.1 = (f32[1024,1152]{1,0:T(8,128)}, f32[1024,1152]{1,0:T(8,128)}, u32[]{:S(2)}, u32[]{:S(2)}) collective-permute-start(f32[1024,1152]{1,0:T(8,128)} %fusion.37), channel_id=1, source_target_pairs={{120,0},{0,8},{8,16},{16,24},{24,32},{32,40},{40,48},{48,56},{56,6... | collective-permute-start | bytes 14155784 | tf_op jit(solution)/shard_map/while/body/eval_jaxpr/ppermute | solution.py:10
  872.6 76.6 %collective-permute-start = (bf16[1024,1152]{1,0:T(8,128)(2,1)S(1)}, bf16[1024,1152]{1,0:T(8,128)(2,1)}, u32[]{:S(2)}, u32[]{:S(2)}) collective-permute-start(bf16[1024,1152]{1,0:T(8,128)(2,1)S(1)} %copy.12), channel_id=1, source_target_pairs={{120,0},{0,8},{8,16},{16,24},{24,32},{32,40},{40,48},{48,56},{56,6... | collective-permute-start | bytes 7077896 | tf_op jit(solution)/shard_map/while/body/eval_jaxpr/ppermute | solution.py:10
  957.7 79.2 %collective-permute-start.1 = (f32[1024,1152]{1,0:T(8,128)}, f32[1024,1152]{1,0:T(8,128)}, u32[]{:S(2)}, u32[]{:S(2)}) collective-permute-start(f32[1024,1152]{1,0:T(8,128)} %fusion.37), channel_id=1, source_target_pairs={{120,0},{0,8},{8,16},{16,24},{24,32},{32,40},{40,48},{48,56},{56,6... | collective-permute-start | bytes 14155784 | tf_op jit(solution)/shard_map/while/body/eval_jaxpr/ppermute | solution.py:10
  1045.5 79.2 %collective-permute-start.1 = (f32[1024,1152]{1,0:T(8,128)}, f32[1024,1152]{1,0:T(8,128)}, u32[]{:S(2)}, u32[]{:S(2)}) collective-permute-start(f32[1024,1152]{1,0:T(8,128)} %fusion.37), channel_id=1, source_target_pairs={{120,0},{0,8},{8,16},{16,24},{24,32},{32,40},{40,48},{48,56},{56,6... | collective-permute-start | bytes 14155784 | tf_op jit(solution)/shard_map/while/body/eval_jaxpr/ppermute | solution.py:10
  1133.2 79.2 %collective-permute-start.1 = (f32[1024,1152]{1,0:T(8,128)}, f32[1024,1152]{1,0:T(8,128)}, u32[]{:S(2)}, u32[]{:S(2)}) collective-permute-start(f32[1024,1152]{1,0:T(8,128)} %fusion.37), channel_id=1, source_target_pairs={{120,0},{0,8},{8,16},{16,24},{24,32},{32,40},{40,48},{48,56},{56,6... | collective-permute-start | bytes 14155784 | tf_op jit(solution)/shard_map/while/body/eval_jaxpr/ppermute | solution.py:10
  1135.8 76.6 %collective-permute-start = (bf16[1024,1152]{1,0:T(8,128)(2,1)S(1)}, bf16[1024,1152]{1,0:T(8,128)(2,1)}, u32[]{:S(2)}, u32[]{:S(2)}) collective-permute-start(bf16[1024,1152]{1,0:T(8,128)(2,1)S(1)} %copy.12), channel_id=1, source_target_pairs={{120,0},{0,8},{8,16},{16,24},{24,32},{32,40},{40,48},{48,56},{56,6... | collective-permute-start | bytes 7077896 | tf_op jit(solution)/shard_map/while/body/eval_jaxpr/ppermute | solution.py:10
  1220.9 79.2 %collective-permute-start.1 = (f32[1024,1152]{1,0:T(8,128)}, f32[1024,1152]{1,0:T(8,128)}, u32[]{:S(2)}, u32[]{:S(2)}) collective-permute-start(f32[1024,1152]{1,0:T(8,128)} %fusion.37), channel_id=1, source_target_pairs={{120,0},{0,8},{8,16},{16,24},{24,32},{32,40},{40,48},{48,56},{56,6... | collective-permute-start | bytes 14155784 | tf_op jit(solution)/shard_map/while/body/eval_jaxpr/ppermute | solution.py:10
  1308.7 79.2 %collective-permute-start.1 = (f32[1024,1152]{1,0:T(8,128)}, f32[1024,1152]{1,0:T(8,128)}, u32[]{:S(2)}, u32[]{:S(2)}) collective-permute-start(f32[1024,1152]{1,0:T(8,128)} %fusion.37), channel_id=1, source_target_pairs={{120,0},{0,8},{8,16},{16,24},{24,32},{32,40},{40,48},{48,56},{56,6... | collective-permute-start | bytes 14155784 | tf_op jit(solution)/shard_map/while/body/eval_jaxpr/ppermute | solution.py:10
  1396.4 79.2 %collective-permute-start.1 = (f32[1024,1152]{1,0:T(8,128)}, f32[1024,1152]{1,0:T(8,128)}, u32[]{:S(2)}, u32[]{:S(2)}) collective-permute-start(f32[1024,1152]{1,0:T(8,128)} %fusion.37), channel_id=1, source_target_pairs={{120,0},{0,8},{8,16},{16,24},{24,32},{32,40},{40,48},{48,56},{56,6... | collective-permute-start | bytes 14155784 | tf_op jit(solution)/shard_map/while/body/eval_jaxpr/ppermute | solution.py:10
  1399.0 76.6 %collective-permute-start = (bf16[1024,1152]{1,0:T(8,128)(2,1)S(1)}, bf16[1024,1152]{1,0:T(8,128)(2,1)}, u32[]{:S(2)}, u32[]{:S(2)}) collective-permute-start(bf16[1024,1152]{1,0:T(8,128)(2,1)S(1)} %copy.12), channel_id=1, source_target_pairs={{120,0},{0,8},{8,16},{16,24},{24,32},{32,40},{40,48},{48,56},{56,6... | collective-permute-start | bytes 7077896 | tf_op jit(solution)/shard_map/while/body/eval_jaxpr/ppermute | solution.py:10
  (16 other events, 883.3 us)
Sparse Core Ops, SparseCore 0:
  10.9 58.7 all-gather.1
  1475.7 116.3 reduce-scatter.1
where the time goes:
time: 1600 us
  waiting for transfers between devices  1380 us (86%)
  matrix products  120 us (8%)
  starting transfers between devices  41.7 us (3%)
  local copies, waits for them, and re-layouts  30.7 us (2%)
    ppermute x32, waiting for transfers between devices, shifted(): return lax.ppermute(block, axis, route)  1210 us
    reduce_scatter x1, waiting for transfers between devices, on_device(): lax.psum_scatter(holder, 'inner', scatter_dimension=0, tiled=True)  112 us
    dot_general x16, matrix products, back_terms(): lax.dot_general(coef, vid_half, (((0,), (0,)), ((), ())), preferred_eleme...  85.3 us
    all_gather x1, waiting for transfers between devices, on_device(): block = lax.all_gather(txt_half, 'inner', axis=0, tiled=True)  53.2 us
    ppermute x32, starting transfers between devices, shifted(): return lax.ppermute(block, axis, route)  41.6 us
  transfers between devices with their start and end apart: 34, of which 18 were waited for; matrix products, arithmetic and copies ran while one was open for 1% of the time, Pallas kernels for 0%

commit v1 on v0

v1 whole, which is shorter than its diff:
```python
import functools

import jax
import jax.numpy as jnp
from jax import lax
from jax.experimental import pallas as pl
from jax.experimental.pallas import tpu as pltpu
from jax.sharding import PartitionSpec as P

MESH = pl.DeviceIdType.MESH
ROWS = 128
HALF = ROWS // 2
PAIR = 2 * ROWS
SLOTS = 8
BLOCKS = 8
EPS = 1e-06

OWN, MATE, UP, DOWN, MATE_UP, MATE_DOWN, FAR, MATE_FAR = range(BLOCKS)


def device_at(x, y, z, core):
    return ((x % 2) * 8 + z * 2 + core, y * 2 + x // 2)


class Places:
    def __init__(self):
        group, inner = lax.axis_index("group"), lax.axis_index("inner")
        core, z, y = group % 2, (group // 2) % 4, inner // 2
        x = (inner % 2) * 2 + group // 8
        odd = x % 2
        self.sibling = device_at(x, y, z, 1 - core)
        self.vid = (
            device_at(x + 1 - 2 * odd, y, z, core),
            device_at(x, (y + 1) % 4, z, core),
            device_at(x, (y + 3) % 4, z, core),
        )
        self.txt = (
            device_at((x + 3 + 2 * odd) % 4, y, z, core),
            device_at(x, y, (z + 1) % 4, core),
            device_at(x, y, (z + 3) % 4, core),
        )

    def all(self):
        return (self.sibling, *self.vid, *self.txt)


GATHER = (
    (0, OWN, MATE, 0),
    (0, OWN, MATE, 1),
    (1, OWN, DOWN, 0),
    (1, OWN, DOWN, 1),
    (2, OWN, UP, 0),
    (2, OWN, UP, 1),
    (1, DOWN, FAR, 0),
    (2, UP, FAR, 1),
    (1, MATE, MATE_DOWN, 0),
    (1, MATE, MATE_DOWN, 1),
    (2, MATE, MATE_UP, 0),
    (2, MATE, MATE_UP, 1),
    (0, FAR, MATE_FAR, 0),
    (0, FAR, MATE_FAR, 1),
)
REDUCE = (
    (0, MATE_FAR, 0),
    (0, MATE_FAR, 1),
    (1, MATE_UP, 0),
    (1, MATE_UP, 1),
    (2, MATE_DOWN, 0),
    (2, MATE_DOWN, 1),
    (2, FAR, 0),
    (1, FAR, 1),
    (0, MATE, 0),
    (0, MATE, 1),
    (1, UP, 0),
    (1, UP, 1),
    (2, DOWN, 0),
    (2, DOWN, 1),
)


class Side:
    def __init__(self, near, blocks, stride, terms, stage, landed, gather_sems, reduce_sems):
        self.near, self.blocks, self.stride = near, blocks, stride
        self.terms, self.stage, self.landed = terms, stage, landed
        self.gather_sems, self.reduce_sems = gather_sems, reduce_sems

    def rows(self, block, half):
        return self.blocks.at[pl.ds(block * self.stride + half * HALF, HALF)]

    def gather(self, i):
        to, source, target, half = GATHER[i]
        return pltpu.make_async_remote_copy(
            src_ref=self.rows(source, half),
            dst_ref=self.rows(target, half),
            send_sem=self.gather_sems.at[0, i],
            recv_sem=self.gather_sems.at[1, i],
            device_id=self.near[to],
            device_id_type=MESH,
        )

    def send(self, *ids):
        for i in ids:
            self.gather(i).start()

    def take(self, *ids):
        for i in ids:
            self.gather(i).wait_recv()

    def reduce(self, i):
        return pltpu.make_async_remote_copy(
            src_ref=self.stage.at[i],
            dst_ref=self.landed.at[i],
            send_sem=self.reduce_sems.at[0, i],
            recv_sem=self.reduce_sems.at[1, i],
            device_id=self.near[REDUCE[i][0]],
            device_id_type=MESH,
        )

    def part(self, block, half):
        return self.terms[pl.ds(block * ROWS + half * HALF, HALF)]

    def give(self, i, *arrived):
        _, block, half = REDUCE[i]
        total = self.part(block, half)
        for j in arrived:
            self.reduce(j).wait_recv()
            total = total + self.landed[j].astype(jnp.float32)
        self.stage[i] = total.astype(jnp.bfloat16)
        self.reduce(i).start()

    def finish(self):
        for i in range(len(GATHER)):
            self.gather(i).wait_send()
        for i in range(len(REDUCE)):
            self.reduce(i).wait_send()


def kernel(
    log_scale_ref, bias_ref, counts_ref, texts_hbm, clips_hbm,
    pool_ref, text_ref,
    texts, clips, vids, txts, coef,
    vid_unit, vid_norm, count_col, txt_unit, txt_norm,
    vid_terms, txt_terms, vid_stage, vid_landed, txt_stage, txt_landed, sib_stage, sib_landed,
    load_sems, vid_gather, vid_reduce, txt_gather, txt_reduce, sib_gather, sib_reduce,
):
    places = Places()
    barrier = pltpu.get_barrier_semaphore()
    for near in places.all():
        pl.semaphore_signal(barrier, inc=1, device_id=near, device_id_type=MESH)
    load_texts = pltpu.make_async_copy(texts_hbm, texts, load_sems.at[0])
    load_clips = pltpu.make_async_copy(clips_hbm, clips, load_sems.at[1])
    load_texts.start()
    load_clips.start()

    vid = Side(places.vid, vids, ROWS, vid_terms, vid_stage, vid_landed, vid_gather, vid_reduce)
    txt = Side(places.txt, txts, PAIR, txt_terms, txt_stage, txt_landed, txt_gather, txt_reduce)

    def to_sibling(block):
        return pltpu.make_async_remote_copy(
            src_ref=txts.at[pl.ds(block * PAIR, ROWS)],
            dst_ref=txts.at[pl.ds(block * PAIR + ROWS, ROWS)],
            send_sem=sib_gather.at[0, block],
            recv_sem=sib_gather.at[1, block],
            device_id=places.sibling,
            device_id_type=MESH,
        )

    def terms_to_sibling(block):
        return pltpu.make_async_remote_copy(
            src_ref=sib_stage.at[block],
            dst_ref=sib_landed.at[block],
            send_sem=sib_reduce.at[0, block],
            recv_sem=sib_reduce.at[1, block],
            device_id=places.sibling,
            device_id_type=MESH,
        )

    scale = jnp.exp(jnp.full((1, 1), log_scale_ref[0], jnp.float32))
    bias = bias_ref[0]

    load_texts.wait()
    text_f = texts[...].astype(jnp.float32)
    norm = jnp.sqrt(jnp.sum(text_f * text_f, axis=1, keepdims=True) + EPS)
    unit = text_f / norm
    txt_unit[...] = unit
    txt_norm[...] = norm
    txts[pl.ds(0, ROWS)] = unit.astype(jnp.bfloat16)

    pl.semaphore_wait(barrier, len(places.all()))
    txt.send(2, 5, 0)
    to_sibling(OWN).start()
    txt.send(3, 4, 1)

    wide = jnp.broadcast_to(counts_ref[...].astype(jnp.float32), (ROWS, ROWS))
    column = jnp.transpose(wide)[:, 0:1]
    count_col[...] = column
    shape = (ROWS, ROWS * SLOTS)
    slot = lax.broadcasted_iota(jnp.int32, shape, 1)
    video = lax.broadcasted_iota(jnp.int32, shape, 0)
    slot = slot - video * SLOTS
    used = jnp.logical_and(slot >= 0, slot.astype(jnp.float32) < column)
    load_clips.wait()
    pooled = jnp.dot(
        used.astype(jnp.float32).astype(jnp.bfloat16), clips[...], preferred_element_type=jnp.float32
    ) / column
    norm = jnp.sqrt(jnp.sum(pooled * pooled, axis=1, keepdims=True) + EPS)
    unit = pooled / norm
    vid_unit[...] = unit
    vid_norm[...] = norm
    vids[pl.ds(0, ROWS)] = unit.astype(jnp.bfloat16)
    vid.send(2, 5, 0, 3, 4, 1)

    def coefs(first, count, block, own=False):
        columns = pl.ds(pl.multiple_of(block * PAIR, PAIR), PAIR)
        dots = lax.dot_general(
            vids[pl.ds(first * ROWS, count * ROWS)],
            txts[columns],
            (((1,), (1,)), ((), ())),
            preferred_element_type=jnp.float32,
        )
        logits = scale * dots + bias
        values = 1.0 / (1.0 + jnp.exp(-logits))
        if own:
            row = lax.broadcasted_iota(jnp.int32, values.shape, 0)
            col = lax.broadcasted_iota(jnp.int32, values.shape, 1)
            values = values - (row == col).astype(jnp.float32)
        coef[pl.ds(first * ROWS, count * ROWS), columns] = values.astype(jnp.bfloat16)

    def coefs_over(first, count, start, stop):
        @pl.loop(start, stop)
        def _(block):
            coefs(first, count, block)

    to_sibling(OWN).wait_recv()
    coefs(0, 1, OWN, own=True)

    for side in (txt, vid):
        side.take(2)
        side.send(6)
        side.take(5)
        side.send(7)
        side.take(0)
        side.send(8, 10)
    for side in (txt, vid):
        side.take(1)
        side.send(9, 11)
    txt.take(3, 4)
    for block in (MATE, UP, DOWN):
        to_sibling(block).start()
    vid.take(3, 4)
    coefs(1, 3, OWN)
    for block in (MATE, UP, DOWN):
        to_sibling(block).wait_recv()
    coefs_over(0, 4, MATE, DOWN)
    for side in (txt, vid):
        side.take(6)
        side.send(12)
        side.take(7)
        side.send(13)
    to_sibling(FAR).start()
    coefs(0, 4, DOWN)
    coefs_over(FAR, 1, OWN, MATE_UP)
    to_sibling(FAR).wait_recv()
    coefs(0, 4, FAR)
    coefs(FAR, 1, FAR)
    txt.take(8, 9, 10, 11)
    to_sibling(MATE_UP).start()
    to_sibling(MATE_DOWN).start()
    vid.take(8, 9, 10, 11)
    coefs_over(MATE_UP, 2, OWN, MATE_UP)
    coefs(MATE_UP, 2, FAR)
    to_sibling(MATE_UP).wait_recv()
    to_sibling(MATE_DOWN).wait_recv()
    coefs_over(0, 7, MATE_UP, FAR)
    txt.take(12, 13)
    to_sibling(MATE_FAR).start()
    vid.take(12, 13)
    coefs_over(MATE_FAR, 1, OWN, MATE_FAR)
    to_sibling(MATE_FAR).wait_recv()
    coefs(0, 8, MATE_FAR)

    def vid_back(first):
        vid_terms[pl.ds(first * ROWS, PAIR)] = jnp.dot(
            coef[pl.ds(first * ROWS, PAIR)], txts[...], preferred_element_type=jnp.float32
        )

    def txt_back(block):
        terms = lax.dot_general(
            coef[:, pl.ds(block * PAIR, PAIR)],
            vids[...],
            (((0,), (0,)), ((), ())),
            preferred_element_type=jnp.float32,
        )
        txt_terms[pl.ds(block * ROWS, ROWS)] = terms[:ROWS]
        sib_stage[block] = terms[ROWS:].astype(jnp.bfloat16)
        terms_to_sibling(block).start()

    def join(block):
        terms_to_sibling(block).wait_recv()
        here = pl.ds(block * ROWS, ROWS)
        txt_terms[here] = txt_terms[here] + sib_landed[block].astype(jnp.float32)

    vid_back(FAR)
    vid.give(0)
    vid.give(1)
    txt_back(MATE_FAR)
    vid_back(MATE_UP)
    for i in (2, 4, 3, 5):
        vid.give(i)
    txt_back(MATE_UP)
    join(MATE_FAR)
    txt.give(0)
    txt.give(1)
    txt_back(MATE_DOWN)
    join(MATE_UP)
    txt.give(2)
    txt.give(3)
    txt_back(FAR)
    join(MATE_DOWN)
    txt.give(4)
    txt.give(5)
    vid_back(OWN)
    vid.give(6, 0)
    vid.give(7, 1)
    vid_back(UP)
    vid.give(10)
    vid.give(13)
    txt_back(MATE)
    join(FAR)
    txt.give(6, 0)
    txt.give(7, 1)
    vid.give(8, 2, 4)
    vid.give(9, 3, 5)
    txt_back(UP)
    vid.give(12, 6)
    vid.give(11, 7)
    txt_back(DOWN)
    join(MATE)
    txt.give(8, 2, 4)
    txt.give(9, 3, 5)
    join(UP)
    txt.give(10)
    join(DOWN)
    txt.give(13)
    txt_back(OWN)
    txt.give(12, 6)
    txt.give(11, 7)

    def total(side, messages):
        for i in messages:
            side.reduce(i).wait_recv()
        top, bottom = (
            side.part(OWN, half)
            + side.landed[8 + half].astype(jnp.float32)
            + side.landed[10 + half].astype(jnp.float32)
            + side.landed[12 + half].astype(jnp.float32)
            for half in (0, 1)
        )
        return scale * jnp.concatenate([top, bottom], axis=0)

    back = total(vid, range(8, 14))
    unit = vid_unit[...]
    back = (back - unit * jnp.sum(unit * back, axis=1, keepdims=True)) / vid_norm[...]
    pool_ref[...] = back / count_col[...]
    join(OWN)
    back = total(txt, range(8, 14))
    unit = txt_unit[...]
    text_ref[...] = (back - unit * jnp.sum(unit * back, axis=1, keepdims=True)) / txt_norm[...]

    vid.finish()
    txt.finish()
    for block in range(BLOCKS):
        to_sibling(block).wait_send()
        terms_to_sibling(block).wait_send()


def on_device(clips, counts, texts, log_scale, bias):
    videos, slots, width = clips.shape
    bf16, f32 = jnp.bfloat16, jnp.float32
    smem = pl.BlockSpec(memory_space=pltpu.SMEM)
    vmem = pl.BlockSpec(memory_space=pltpu.VMEM)
    hbm = pl.BlockSpec(memory_space=pl.ANY)
    dma = pltpu.SemaphoreType.DMA
    own = jax.ShapeDtypeStruct((videos, width), f32)
    pool_grad, text_grad = pl.pallas_call(
        kernel,
        out_shape=(own, own),
        in_specs=[smem, smem, vmem, hbm, hbm],
        out_specs=(vmem, vmem),
        scratch_shapes=[
            pltpu.VMEM((ROWS, width), bf16),
            pltpu.VMEM((ROWS * SLOTS, width), bf16),
            pltpu.VMEM((BLOCKS * ROWS, width), bf16),
            pltpu.VMEM((BLOCKS * PAIR, width), bf16),
            pltpu.VMEM((BLOCKS * ROWS, BLOCKS * PAIR), bf16),
            pltpu.VMEM((ROWS, width), f32),
            pltpu.VMEM((ROWS, 1), f32),
            pltpu.VMEM((ROWS, 1), f32),
            pltpu.VMEM((ROWS, width), f32),
            pltpu.VMEM((ROWS, 1), f32),
            pltpu.VMEM((BLOCKS * ROWS, width), f32),
            pltpu.VMEM((BLOCKS * ROWS, width), f32),
            pltpu.VMEM((len(REDUCE), HALF, width), bf16),
            pltpu.VMEM((len(REDUCE), HALF, width), bf16),
            pltpu.VMEM((len(REDUCE), HALF, width), bf16),
            pltpu.VMEM((len(REDUCE), HALF, width), bf16),
            pltpu.VMEM((BLOCKS, ROWS, width), bf16),
            pltpu.VMEM((BLOCKS, ROWS, width), bf16),
            dma((2,)),
            dma((2, len(GATHER))),
            dma((2, len(REDUCE))),
            dma((2, len(GATHER))),
            dma((2, len(REDUCE))),
            dma((2, BLOCKS)),
            dma((2, BLOCKS)),
        ],
        compiler_params=pltpu.CompilerParams(
            collective_id=0, has_side_effects=True, vmem_limit_bytes=60 * 1024 * 1024
        ),
        cost_estimate=pl.CostEstimate(
            flops=6 * 1024 * 2048 * width, bytes_accessed=4 * 1024 * 1024, transcendentals=2 * 1024 * 2048
        ),
    )(log_scale, bias, counts.reshape(1, videos), texts, clips.reshape(videos * slots, width))
    slot_ids = lax.broadcasted_iota(jnp.int32, (videos, slots), 1)
    used = (slot_ids < counts[:, None]).astype(f32)
    return pool_grad[:, None, :] * used[:, :, None], text_grad


def solution(mesh):
    return jax.shard_map(
        on_device,
        mesh=mesh,
        in_specs=(
            P(("group", "inner"), None, None),
            P(("group", "inner")),
            P(("group", "inner"), None),
            P(),
            P(),
        ),
        out_specs=(P(("group", "inner"), None, None), P(("group", "inner"), None)),
        check_vma=False,
    )
```

time: 1600 us -> 70.5 us (0.04)
  waiting for transfers between devices: 1380 us -> 0 us
  matrix products: 120 us -> 0 us
  Pallas kernels: 0 us -> 63.1 us
  starting transfers between devices: 41.7 us -> 0 us
  local copies, waits for them, and re-layouts: 30.7 us -> 0.82 us
    ppermute x32 -> x0, waiting for transfers between devices: 1210 us -> none  [shifted(): return lax.ppermute(block, axis, route)]
    dot_general x48 -> x0, matrix products: 120 us -> none  [the longest x16 85.3 us: back_terms(): lax.dot_general(coef, vid_half, (((0,), (0,)), ((), ())), preferred_eleme...]
    reduce_scatter x1 -> x0, waiting for transfers between devices: 112 us -> none  [on_device(): lax.psum_scatter(holder, 'inner', scatter_dimension=0, tiled=True)]
    pallas_call x0 -> x1, Pallas kernels: none -> 63.1 us  [on_device(): pl.pallas_call(kernel, out_shape=(own, own), in_specs=[smem, smem, vmem,...]
    all_gather x1 -> x0, waiting for transfers between devices: 53.2 us -> none  [on_device(): block = lax.all_gather(txt_half, 'inner', axis=0, tiled=True)]
    ppermute x32 -> x0, starting transfers between devices: 41.6 us -> none  [shifted(): return lax.ppermute(block, axis, route)]
    while x16 -> x0, local copies, waits for them, and re-layouts: 26.7 us -> none
  transfers between devices with their start and end apart: 34 -> 0, of which waited for: 18 -> 0; matrix products, arithmetic and copies ran while one was open for 1% -> 0% of each run, Pallas kernels for 0% -> 0%
where the time goes in v1:
time: 70.5 us; the launch traced here: 70.3 us
  Pallas kernels  63.1 us (90%)
  other arithmetic  4.43 us (6%)
  between operations  1.95 us (3%)
  local copies, waits for them, and re-layouts  0.82 us (1%)
    pallas_call x1, Pallas kernels, on_device(): pl.pallas_call(kernel, out_shape=(own, own), in_specs=[smem, smem, vmem,...  63.1 us
    mul x1, other arithmetic, on_device(): return (pool_grad[:, None, :] * used[:, :, None], text_grad)  3.7 us

profile of v1, /device:TPU:1, one launch (start us, length us, event | category | flops | bytes accessed | tf_op | source)
XLA Modules:
  0.0 70.3 jit_solution(6395492127021223649)
XLA Ops:
  1.9 0.7 %fusion = f32[128,8]{1,0:T(8,128)S(1)} fusion(s32[128]{0:T(128)} %param.6), kind=kLoop, calls=%fused_computation.2 | loop fusion | flops 2048 | bytes 4608 | tf_op jit(solution)/shard_map/convert_element_type | solution.py:425
  2.7 63.1 %shard_map.68 = (f32[128,1152]{1,0:T(8,128)}, f32[128,1152]{1,0:T(8,128)}) custom-call(f32[1]{0:T(128)S(6)} %copy.8.log_scale_ref, f32[1]{0:T(128)S(6)} %copy.9.bias_ref, s32[1,128]{1,0:T(1,128)} %bitcast.2, bf16[128,1152]{1,0:T(8,128)(2,1)} %texts_hbm.1, bf16[1024,1152]{1,0:T(8,128)(2,1)} %bitcast.3), custom_call_target="tpu_custom_call" | custom-call | flops 14495514624 | bytes 4194304 | tf_op jit(solution)/shard_map/pallas_call | solution.py:385
  65.8 0.0 copy-start
  65.8 3.7 %broadcast_multiply_fusion = f32[128,8,1152]{2,1,0:T(8,128)} fusion(f32[128,8]{1,0:T(8,128)S(1)} %fusion, f32[128,1152]{1,0:T(8,128)} %get-tuple-element.4), kind=kLoop, calls=%fused_computation | loop fusion | flops 1179648 | bytes 5312512 | tf_op jit(solution)/shard_map/mul | solution.py:426
  69.5 0.0 copy-done
  69.5 0.8 %copy.10 = f32[128,1152]{1,0:T(8,128)} copy(f32[128,1152]{1,0:T(8,128)S(1)} %copy-done) | data formatting | bytes 1179648
Async XLA Ops:
  65.8 3.7 %copy-start = (f32[128,1152]{1,0:T(8,128)S(1)}, f32[128,1152]{1,0:T(8,128)}, u32[]{:S(2)}) copy-start(f32[128,1152]{1,0:T(8,128)} %get-tuple-element.9) | copy-start | bytes 1769476

commit v2 on v1

v2 whole, which is shorter than its diff:
```python
import functools

import jax
import jax.numpy as jnp
from jax import lax
from jax.experimental import pallas as pl
from jax.experimental.pallas import tpu as pltpu
from jax.sharding import PartitionSpec as P

MESH = pl.DeviceIdType.MESH
ROWS = 128
SLOTS = 8
BLOCKS = 8
EPS = 1e-06

OWN, MATE, UP, DOWN, FAR = ((i * ROWS, ROWS) for i in range(5))
MATE_UP = ((640, 64), (768, 64))
MATE_DOWN = ((704, 64), (832, 64))
MATE_FAR = (896, ROWS)
PIECES = (OWN, MATE, UP, DOWN, FAR, MATE_UP[0], MATE_DOWN[0], MATE_UP[1], MATE_DOWN[1], MATE_FAR)
EARLY, MIDDLE, ALL = 640, 768, 1024


def device_at(x, y, z, core):
    return ((x % 2) * 8 + z * 2 + core, y * 2 + x // 2)


class Places:
    def __init__(self):
        group, inner = lax.axis_index("group"), lax.axis_index("inner")
        core, z, y = group % 2, (group // 2) % 4, inner // 2
        x = (inner % 2) * 2 + group // 8
        odd = x % 2
        self.sibling = device_at(x, y, z, 1 - core)
        self.vid = (
            device_at(x + 1 - 2 * odd, y, z, core),
            device_at(x, (y + 1) % 4, z, core),
            device_at(x, (y + 3) % 4, z, core),
        )
        self.txt = (
            device_at((x + 3 + 2 * odd) % 4, y, z, core),
            device_at(x, y, (z + 1) % 4, core),
            device_at(x, y, (z + 3) % 4, core),
        )

    def all(self):
        return (self.sibling, *self.vid, *self.txt)


GATHER = (
    *((1, OWN, DOWN, row, rows) for row, rows in ((0, 32), (32, 32), (64, 64))),
    *((2, OWN, UP, row, rows) for row, rows in ((64, 32), (96, 32), (0, 64))),
    *((0, OWN, MATE, row, 64) for row in (0, 64)),
    *((1, DOWN, FAR, row, 32) for row in (0, 32)),
    *((2, UP, FAR, row, 32) for row in (64, 96)),
    *((1, MATE, MATE_DOWN, row, 64) for row in (0, 64)),
    *((2, MATE, MATE_UP, row, 64) for row in (0, 64)),
    *((0, FAR, MATE_FAR, row, 32) for row in (0, 64, 32, 96)),
)
REDUCE = (
    *((0, MATE_FAR, row, 32) for row in (0, 64, 32, 96)),
    *((1, MATE_UP[half], 0, 64) for half in (0, 1)),
    *((2, MATE_DOWN[half], 0, 64) for half in (0, 1)),
    (1, UP, 0, 64),
    (2, DOWN, 64, 64),
    *((2, FAR, row, 32) for row in (0, 32)),
    *((1, FAR, row, 32) for row in (64, 96)),
    *((0, MATE, row, 64) for row in (0, 64)),
    *((1, UP, row, 32) for row in (64, 96)),
    *((2, DOWN, row, 32) for row in (0, 32)),
)
PLACE = tuple(sum(message[3] for message in REDUCE[:i]) for i in range(len(REDUCE)))


class Side:
    def __init__(self, cores, near, blocks, terms, stage, landed, gather_sems, reduce_sems):
        self.cores, self.near, self.blocks = cores, near, blocks
        self.terms, self.stage, self.landed = terms, stage, landed
        self.gather_sems, self.reduce_sems = gather_sems, reduce_sems

    def rows(self, piece, row, rows):
        if isinstance(piece[0], tuple):
            piece, row = piece[row // 64], row % 64
        return pl.ds(self.cores * piece[0] + row, rows)

    def gather(self, i):
        to, source, target, row, rows = GATHER[i]
        return pltpu.make_async_remote_copy(
            src_ref=self.blocks.at[self.rows(source, row, rows)],
            dst_ref=self.blocks.at[self.rows(target, row, rows)],
            send_sem=self.gather_sems.at[0, i],
            recv_sem=self.gather_sems.at[1, i],
            device_id=self.near[to],
            device_id_type=MESH,
        )

    def send(self, *ids):
        for i in ids:
            self.gather(i).start()

    def take(self, *ids):
        for i in ids:
            self.gather(i).wait_recv()

    def place(self, i):
        return pl.ds(PLACE[i], REDUCE[i][3])

    def reduce(self, i):
        here = self.place(i)
        return pltpu.make_async_remote_copy(
            src_ref=self.stage.at[here],
            dst_ref=self.landed.at[here],
            send_sem=self.reduce_sems.at[0, i],
            recv_sem=self.reduce_sems.at[1, i],
            device_id=self.near[REDUCE[i][0]],
            device_id_type=MESH,
        )

    def arrived(self, i):
        self.reduce(i).wait_recv()
        return self.landed[self.place(i)].astype(jnp.float32)

    def give(self, i, *others):
        _, piece, row, rows = REDUCE[i]
        total = self.terms[self.rows(piece, row, rows)]
        for j in others:
            total = total + self.arrived(j)
        self.stage[self.place(i)] = total.astype(jnp.bfloat16)
        self.reduce(i).start()

    def own(self):
        top = self.terms[self.rows(OWN, 0, 64)] + self.arrived(8) + self.arrived(14)
        top = top + jnp.concatenate([self.arrived(18), self.arrived(19)], axis=0)
        bottom = self.terms[self.rows(OWN, 64, 64)] + self.arrived(9) + self.arrived(15)
        bottom = bottom + jnp.concatenate([self.arrived(16), self.arrived(17)], axis=0)
        return jnp.concatenate([top, bottom], axis=0)

    def finish(self):
        for i in range(len(GATHER)):
            self.gather(i).wait_send()
        for i in range(len(REDUCE)):
            self.reduce(i).wait_send()


def kernel(
    log_scale_ref, bias_ref, counts_ref, texts_hbm, clips_hbm,
    pool_ref, text_ref,
    texts, clips, vids, txts, coef,
    vid_unit, vid_norm, count_col, txt_unit, txt_norm,
    vid_terms, txt_terms, vid_stage, vid_landed, txt_stage, txt_landed, sib_stage, sib_landed,
    load_sems, vid_gather, vid_reduce, txt_gather, txt_reduce, sib_gather, sib_reduce,
):
    places = Places()
    barrier = pltpu.get_barrier_semaphore()
    for near in places.all():
        pl.semaphore_signal(barrier, inc=1, device_id=near, device_id_type=MESH)
    load_texts = pltpu.make_async_copy(texts_hbm, texts, load_sems.at[0])
    load_clips = pltpu.make_async_copy(clips_hbm, clips, load_sems.at[1])
    load_texts.start()
    load_clips.start()

    vid = Side(1, places.vid, vids, vid_terms, vid_stage, vid_landed, vid_gather, vid_reduce)
    txt = Side(2, places.txt, txts, txt_terms, txt_stage, txt_landed, txt_gather, txt_reduce)

    def to_sibling(piece):
        first, rows = piece
        return pltpu.make_async_remote_copy(
            src_ref=txts.at[pl.ds(2 * first, rows)],
            dst_ref=txts.at[pl.ds(2 * first + rows, rows)],
            send_sem=sib_gather.at[0, PIECES.index(piece)],
            recv_sem=sib_gather.at[1, PIECES.index(piece)],
            device_id=places.sibling,
            device_id_type=MESH,
        )

    def terms_to_sibling(piece):
        return pltpu.make_async_remote_copy(
            src_ref=sib_stage.at[pl.ds(*piece)],
            dst_ref=sib_landed.at[pl.ds(*piece)],
            send_sem=sib_reduce.at[0, PIECES.index(piece)],
            recv_sem=sib_reduce.at[1, PIECES.index(piece)],
            device_id=places.sibling,
            device_id_type=MESH,
        )

    scale = jnp.exp(jnp.full((1, 1), log_scale_ref[0], jnp.float32))
    bias = bias_ref[0]

    load_texts.wait()
    text_f = texts[...].astype(jnp.float32)
    norm = jnp.sqrt(jnp.sum(text_f * text_f, axis=1, keepdims=True) + EPS)
    unit = text_f / norm
    txt_unit[...] = unit
    txt_norm[...] = norm
    txts[pl.ds(0, ROWS)] = unit.astype(jnp.bfloat16)

    wide = jnp.broadcast_to(counts_ref[...].astype(jnp.float32), (ROWS, ROWS))
    column = jnp.transpose(wide)[:, 0:1]
    count_col[...] = column
    shape = (ROWS, ROWS * SLOTS)
    slot = lax.broadcasted_iota(jnp.int32, shape, 1)
    video = lax.broadcasted_iota(jnp.int32, shape, 0)
    slot = slot - video * SLOTS
    used = jnp.logical_and(slot >= 0, slot.astype(jnp.float32) < column)
    load_clips.wait()
    pooled = jnp.dot(
        used.astype(jnp.float32).astype(jnp.bfloat16), clips[...], preferred_element_type=jnp.float32
    ) / column
    norm = jnp.sqrt(jnp.sum(pooled * pooled, axis=1, keepdims=True) + EPS)
    unit = pooled / norm
    vid_unit[...] = unit
    vid_norm[...] = norm
    vids[pl.ds(0, ROWS)] = unit.astype(jnp.bfloat16)

    pl.semaphore_wait(barrier, len(places.all()))
    for side in (txt, vid):
        side.send(0, 3, 6)
    to_sibling(OWN).start()
    for side in (txt, vid):
        side.send(1, 4, 2, 5, 7)

    def coefs(first, stop, left, right, own=False):
        rows, columns = pl.ds(first, stop - first), pl.ds(left, right - left)
        dots = lax.dot_general(
            vids[rows], txts[columns], (((1,), (1,)), ((), ())), preferred_element_type=jnp.float32
        )
        logits = scale * dots + bias
        values = 1.0 / (1.0 + jnp.exp(-logits))
        if own:
            row = lax.broadcasted_iota(jnp.int32, (ROWS, ROWS), 0)
            col = lax.broadcasted_iota(jnp.int32, (ROWS, ROWS), 1)
            corner = values[:ROWS, :ROWS] - (row == col).astype(jnp.float32)
            coef[pl.ds(0, ROWS), pl.ds(0, ROWS)] = corner.astype(jnp.bfloat16)
            coef[pl.ds(0, ROWS), pl.ds(ROWS, right - ROWS)] = values[:ROWS, ROWS:].astype(jnp.bfloat16)
            coef[pl.ds(ROWS, stop - ROWS), columns] = values[ROWS:].astype(jnp.bfloat16)
        else:
            coef[rows, columns] = values.astype(jnp.bfloat16)

    def vid_back(first, stop, left, right, add=False):
        rows, columns = pl.ds(first, stop - first), pl.ds(left, right - left)
        terms = jnp.dot(coef[rows, columns], txts[columns], preferred_element_type=jnp.float32)
        vid_terms[rows] = vid_terms[rows] + terms if add else terms

    def txt_back(left, right, first, stop, add=False):
        rows, columns = pl.ds(first, stop - first), pl.ds(left, right - left)
        terms = lax.dot_general(
            coef[rows, columns], vids[rows], (((0,), (0,)), ((), ())), preferred_element_type=jnp.float32
        )
        txt_terms[columns] = txt_terms[columns] + terms if add else terms

    def hand_over(*pieces):
        for piece in pieces:
            first, rows = piece
            sib_stage[pl.ds(*piece)] = txt_terms[pl.ds(2 * first + rows, rows)].astype(jnp.bfloat16)
            terms_to_sibling(piece).start()

    def join(*pieces):
        for piece in pieces:
            first, rows = piece
            terms_to_sibling(piece).wait_recv()
            here = pl.ds(2 * first, rows)
            txt_terms[here] = txt_terms[here] + sib_landed[pl.ds(*piece)].astype(jnp.float32)

    sides = (txt, vid)
    early, middle, every = 2 * EARLY, 2 * MIDDLE, 2 * ALL

    for first, second in ((0, 8), (3, 10), (1, 9), (4, 11)):
        for side in sides:
            side.take(first)
            side.send(second)
    for side in sides:
        side.take(6)
        side.send(12, 14)
    for side in sides:
        side.take(7)
        side.send(13, 15)
    to_sibling(MATE).start()
    txt.take(2, 5)
    to_sibling(UP).start()
    to_sibling(DOWN).start()
    vid.take(2, 5)
    to_sibling(OWN).wait_recv()
    to_sibling(MATE).wait_recv()
    coefs(0, 512, 0, 512, own=True)
    for first, second in ((8, 16), (10, 17), (9, 18), (11, 19)):
        for side in sides:
            side.take(first)
            side.send(second)
    to_sibling(FAR).start()
    to_sibling(UP).wait_recv()
    to_sibling(DOWN).wait_recv()
    coefs(0, 512, 512, 1024)
    vid_back(0, 512, 0, 1024)
    txt.take(12, 14)
    to_sibling(MATE_UP[0]).start()
    to_sibling(MATE_DOWN[0]).start()
    vid.take(12, 14)
    txt_back(0, 1024, 0, 512)
    to_sibling(FAR).wait_recv()
    coefs(512, MIDDLE, 0, 1024)
    to_sibling(MATE_UP[0]).wait_recv()
    to_sibling(MATE_DOWN[0]).wait_recv()
    coefs(0, MIDDLE, 1024, middle)
    txt.take(13, 15, 16, 17, 18, 19)
    for piece in (MATE_UP[1], MATE_DOWN[1], MATE_FAR):
        to_sibling(piece).start()
    vid.take(13, 15, 16, 17, 18, 19)

    coefs(MIDDLE, ALL, 0, middle)
    txt_back(early, middle, 0, ALL)
    hand_over(MATE_UP[0], MATE_DOWN[0])
    for piece in (MATE_UP[1], MATE_DOWN[1], MATE_FAR):
        to_sibling(piece).wait_recv()
    coefs(EARLY, ALL, middle, every)
    vid_back(EARLY, MIDDLE, 0, every)
    vid.give(4)
    vid.give(6)
    join(MATE_UP[0], MATE_DOWN[0])
    txt.give(4)
    txt.give(6)
    coefs(0, EARLY, middle, every)
    txt_back(middle, every, 0, ALL)
    hand_over(MATE_FAR, MATE_UP[1], MATE_DOWN[1])
    vid_back(MIDDLE, ALL, 0, every)
    for i in (0, 1, 2, 3, 5, 7):
        vid.give(i)
    join(MATE_FAR, MATE_UP[1], MATE_DOWN[1])
    for i in (0, 1, 2, 3, 5, 7):
        txt.give(i)
    vid_back(0, 512, 1024, every, add=True)
    vid.give(8)
    vid.give(9)
    txt_back(0, 1024, 512, ALL, add=True)
    hand_over(UP, DOWN, MATE, OWN)
    vid_back(512, EARLY, 0, every)
    for i, other in ((10, 0), (12, 1), (11, 2), (13, 3)):
        vid.give(i, other)
    txt_back(1024, early, 0, ALL)
    hand_over(FAR)
    join(UP, DOWN)
    txt.give(8)
    txt.give(9)
    join(FAR)
    for i, other in ((10, 0), (12, 1), (11, 2), (13, 3)):
        txt.give(i, other)
    vid.give(14, 4, 6)
    vid.give(15, 5, 7)
    join(MATE)
    txt.give(14, 4, 6)
    txt.give(15, 5, 7)
    for i, other in ((18, 10), (16, 12), (19, 11), (17, 13)):
        vid.give(i, other)
    for i, other in ((18, 10), (16, 12), (19, 11), (17, 13)):
        txt.give(i, other)

    back = scale * vid.own()
    unit = vid_unit[...]
    back = (back - unit * jnp.sum(unit * back, axis=1, keepdims=True)) / vid_norm[...]
    pool_ref[...] = back / count_col[...]
    join(OWN)
    back = scale * txt.own()
    unit = txt_unit[...]
    text_ref[...] = (back - unit * jnp.sum(unit * back, axis=1, keepdims=True)) / txt_norm[...]

    vid.finish()
    txt.finish()
    for piece in PIECES:
        to_sibling(piece).wait_send()
        terms_to_sibling(piece).wait_send()


def spread(counts_ref, pool_hbm, text_hbm, clip_hbm, text_out, pool, text, clip, load_sems, store_sems):
    videos, slots, width = clip.shape
    parts = store_sems.shape[0] - 1
    step = videos // parts
    load_text = pltpu.make_async_copy(text_hbm, text, load_sems.at[parts])
    store_text = pltpu.make_async_copy(text, text_out, store_sems.at[parts])

    def part(i):
        return pl.ds(i * step, step)

    def load(i):
        return pltpu.make_async_copy(pool_hbm.at[part(i)], pool.at[part(i)], load_sems.at[i])

    def store(i):
        return pltpu.make_async_copy(clip.at[part(i)], clip_hbm.at[part(i)], store_sems.at[i])

    for i in range(parts):
        load(i).start()
    load_text.start()
    slot = lax.broadcasted_iota(jnp.int32, (slots, width), 0)
    for i in range(parts):
        load(i).wait()
        for video in range(i * step, (i + 1) * step):
            row = jnp.broadcast_to(pool[pl.ds(video, 1)], (slots, width))
            clip[video] = jnp.where(slot < counts_ref[video], row, 0.0)
        store(i).start()
    load_text.wait()
    store_text.start()
    for i in range(parts):
        store(i).wait()
    store_text.wait()


def on_device(clips, counts, texts, log_scale, bias):
    videos, slots, width = clips.shape
    bf16, f32 = jnp.bfloat16, jnp.float32
    smem = pl.BlockSpec(memory_space=pltpu.SMEM)
    vmem = pl.BlockSpec(memory_space=pltpu.VMEM)
    hbm = pl.BlockSpec(memory_space=pl.ANY)
    dma = pltpu.SemaphoreType.DMA
    own = jax.ShapeDtypeStruct((videos, width), f32)
    pool_grad, text_grad = pl.pallas_call(
        kernel,
        out_shape=(own, own),
        in_specs=[smem, smem, vmem, hbm, hbm],
        out_specs=(vmem, vmem),
        scratch_shapes=[
            pltpu.VMEM((ROWS, width), bf16),
            pltpu.VMEM((ROWS * SLOTS, width), bf16),
            pltpu.VMEM((BLOCKS * ROWS, width), bf16),
            pltpu.VMEM((2 * BLOCKS * ROWS, width), bf16),
            pltpu.VMEM((BLOCKS * ROWS, 2 * BLOCKS * ROWS), bf16),
            pltpu.VMEM((ROWS, width), f32),
            pltpu.VMEM((ROWS, 1), f32),
            pltpu.VMEM((ROWS, 1), f32),
            pltpu.VMEM((ROWS, width), f32),
            pltpu.VMEM((ROWS, 1), f32),
            pltpu.VMEM((BLOCKS * ROWS, width), f32),
            pltpu.VMEM((2 * BLOCKS * ROWS, width), f32),
            pltpu.VMEM(((BLOCKS - 1) * ROWS, width), bf16),
            pltpu.VMEM(((BLOCKS - 1) * ROWS, width), bf16),
            pltpu.VMEM(((BLOCKS - 1) * ROWS, width), bf16),
            pltpu.VMEM(((BLOCKS - 1) * ROWS, width), bf16),
            pltpu.VMEM((BLOCKS * ROWS, width), bf16),
            pltpu.VMEM((BLOCKS * ROWS, width), bf16),
            dma((2,)),
            dma((2, len(GATHER))),
            dma((2, len(REDUCE))),
            dma((2, len(GATHER))),
            dma((2, len(REDUCE))),
            dma((2, len(PIECES))),
            dma((2, len(PIECES))),
        ],
        compiler_params=pltpu.CompilerParams(
            collective_id=0, has_side_effects=True, vmem_limit_bytes=60 * 1024 * 1024
        ),
        cost_estimate=pl.CostEstimate(
            flops=6 * 1024 * 2048 * width, bytes_accessed=4 * 1024 * 1024, transcendentals=2 * 1024 * 2048
        ),
    )(log_scale, bias, counts.reshape(1, videos), texts, clips.reshape(videos * slots, width))
    return pl.pallas_call(
        spread,
        out_shape=(jax.ShapeDtypeStruct((videos, slots, width), f32), own),
        in_specs=[smem, hbm, hbm],
        out_specs=(hbm, hbm),
        scratch_shapes=[
            pltpu.VMEM((videos, width), f32),
            pltpu.VMEM((videos, width), f32),
            pltpu.VMEM((videos, slots, width), f32),
            dma((5,)),
            dma((5,)),
        ],
        compiler_params=pltpu.CompilerParams(vmem_limit_bytes=60 * 1024 * 1024),
        cost_estimate=pl.CostEstimate(flops=0, bytes_accessed=6 * 1024 * 1024, transcendentals=0),
    )(counts, pool_grad, text_grad)


def solution(mesh):
    return jax.shard_map(
        on_device,
        mesh=mesh,
        in_specs=(
            P(("group", "inner"), None, None),
            P(("group", "inner")),
            P(("group", "inner"), None),
            P(),
            P(),
        ),
        out_specs=(P(("group", "inner"), None, None), P(("group", "inner"), None)),
        check_vma=False,
    )
```

time: 70.5 us -> 67.2 us (0.953)
  the two profiles are of different devices: /device:TPU:1 before, /device:TPU:0 now
where the time goes in v2:
time: 67.2 us; the launch traced here: 67 us
  Pallas kernels  64.9 us (97%)
  between operations  2.09 us (3%)
    pallas_call x1, Pallas kernels, on_device(): pl.pallas_call(kernel, out_shape=(own, own), in_specs=[smem, smem, vmem,...  60.8 us
    pallas_call x1, Pallas kernels, on_device(): pl.pallas_call(spread, out_shape=(jax.ShapeDtypeStruct((videos, slots, wi...  4.15 us

profile of v2, /device:TPU:0, one launch (start us, length us, event | category | flops | bytes accessed | tf_op | source)
XLA Modules:
  0.0 67.0 jit_solution(16922157438748672312)
XLA Ops:
  1.9 60.8 %shard_map.68 = (f32[128,1152]{1,0:T(8,128)}, f32[128,1152]{1,0:T(8,128)}) custom-call(f32[1]{0:T(128)S(6)} %copy.7.log_scale_ref, f32[1]{0:T(128)S(6)} %copy.8.bias_ref, s32[1,128]{1,0:T(1,128)} %bitcast.2, bf16[128,1152]{1,0:T(8,128)(2,1)} %texts_hbm.1, bf16[1024,1152]{1,0:T(8,128)(2,1)} %bitcast.3), custom_call_target="tpu_custom_call" | custom-call | flops 14495514624 | bytes 4194304 | tf_op jit(solution)/shard_map/pallas_call | solution.py:413
  62.7 4.2 %shard_map.69 = (f32[128,8,1152]{2,1,0:T(8,128)}, f32[128,1152]{1,0:T(8,128)}) custom-call(s32[128]{0:T(128)} %counts_ref.1, f32[128,1152]{1,0:T(8,128)} %get-tuple-element.4.pool_hbm, f32[128,1152]{1,0:T(8,128)} %get-tuple-element.5.text_hbm), custom_call_target="tpu_custom_call" | custom-call | bytes 6291456 | tf_op jit(solution)/shard_map/pallas_call | solution.py:452

commit v3 on v2

--- a/solution.py
+++ b/solution.py
@@ -18,7 +18,7 @@
 MATE_DOWN = ((704, 64), (832, 64))
 MATE_FAR = (896, ROWS)
 PIECES = (OWN, MATE, UP, DOWN, FAR, MATE_UP[0], MATE_DOWN[0], MATE_UP[1], MATE_DOWN[1], MATE_FAR)
-EARLY, MIDDLE, ALL = 640, 768, 1024
+EARLY, MIDDLE, FIRST, ALL = 640, 768, 896, 1024
 
 
 def device_at(x, y, z, core):
@@ -281,8 +281,12 @@
     vid.take(2, 5)
     to_sibling(OWN).wait_recv()
     to_sibling(MATE).wait_recv()
+    for first, second in ((8, 16), (10, 17)):
+        for side in sides:
+            side.take(first)
+            side.send(second)
     coefs(0, 512, 0, 512, own=True)
-    for first, second in ((8, 16), (10, 17), (9, 18), (11, 19)):
+    for first, second in ((9, 18), (11, 19)):
         for side in sides:
             side.take(first)
             side.send(second)
@@ -318,40 +322,49 @@
     join(MATE_UP[0], MATE_DOWN[0])
     txt.give(4)
     txt.give(6)
+    vid_back(FIRST, ALL, 0, every)
+    for i in (0, 1, 2, 3):
+        vid.give(i)
     coefs(0, EARLY, middle, every)
-    txt_back(middle, every, 0, ALL)
-    hand_over(MATE_FAR, MATE_UP[1], MATE_DOWN[1])
-    vid_back(MIDDLE, ALL, 0, every)
-    for i in (0, 1, 2, 3, 5, 7):
-        vid.give(i)
-    join(MATE_FAR, MATE_UP[1], MATE_DOWN[1])
-    for i in (0, 1, 2, 3, 5, 7):
+    txt_back(2 * FIRST, every, 0, ALL)
+    hand_over(MATE_FAR)
+    txt_back(middle, 2 * FIRST, 0, ALL)
+    hand_over(MATE_UP[1], MATE_DOWN[1])
+    join(MATE_FAR)
+    for i in (0, 1, 2, 3):
         txt.give(i)
+    vid_back(MIDDLE, FIRST, 0, every)
+    vid.give(5)
+    vid.give(7)
+    join(MATE_UP[1], MATE_DOWN[1])
+    txt.give(5)
+    txt.give(7)
+    txt_back(512, 1024, 512, ALL, add=True)
+    txt_back(1024, early, 0, ALL)
+    hand_over(UP, DOWN, FAR)
+    vid_back(512, EARLY, 0, every)
     vid_back(0, 512, 1024, every, add=True)
+    join(UP, DOWN, FAR)
+    for i, other in ((10, 0), (12, 1), (11, 2), (13, 3)):
+        vid.give(i, other)
     vid.give(8)
     vid.give(9)
-    txt_back(0, 1024, 512, ALL, add=True)
-    hand_over(UP, DOWN, MATE, OWN)
-    vid_back(512, EARLY, 0, every)
-    for i, other in ((10, 0), (12, 1), (11, 2), (13, 3)):
-        vid.give(i, other)
-    txt_back(1024, early, 0, ALL)
-    hand_over(FAR)
-    join(UP, DOWN)
+    txt.give(10, 0)
+    txt.give(12, 1)
     txt.give(8)
     txt.give(9)
-    join(FAR)
-    for i, other in ((10, 0), (12, 1), (11, 2), (13, 3)):
-        txt.give(i, other)
+    txt_back(0, 512, 512, ALL, add=True)
+    hand_over(MATE, OWN)
     vid.give(14, 4, 6)
     vid.give(15, 5, 7)
+    txt.give(11, 2)
+    txt.give(13, 3)
     join(MATE)
     txt.give(14, 4, 6)
     txt.give(15, 5, 7)
     for i, other in ((18, 10), (16, 12), (19, 11), (17, 13)):
-        vid.give(i, other)
-    for i, other in ((18, 10), (16, 12), (19, 11), (17, 13)):
-        txt.give(i, other)
+        for side in (vid, txt):
+            side.give(i, other)
 
     back = scale * vid.own()
     unit = vid_unit[...]

time: 67.2 us -> 63.9 us (0.951)
  the two profiles are of different devices: /device:TPU:0 before, /device:TPU:1 now
where the time goes in v3:
time: 63.9 us; the launch traced here: 63.7 us
  Pallas kernels  61.6 us (96%)
  between operations  2.09 us (3%)
    pallas_call x1, Pallas kernels, on_device(): pl.pallas_call(kernel, out_shape=(own, own), in_specs=[smem, smem, vmem,...  57.4 us
    pallas_call x1, Pallas kernels, on_device(): pl.pallas_call(spread, out_shape=(jax.ShapeDtypeStruct((videos, slots, wi...  4.15 us

profile of v3, /device:TPU:1, one launch (start us, length us, event | category | flops | bytes accessed | tf_op | source)
XLA Modules:
  0.0 63.7 jit_solution(10737378464629681663)
XLA Ops:
  1.9 57.4 %shard_map.68 = (f32[128,1152]{1,0:T(8,128)}, f32[128,1152]{1,0:T(8,128)}) custom-call(f32[1]{0:T(128)S(6)} %copy.7.log_scale_ref, f32[1]{0:T(128)S(6)} %copy.8.bias_ref, s32[1,128]{1,0:T(1,128)} %bitcast.2, bf16[128,1152]{1,0:T(8,128)(2,1)} %texts_hbm.1, bf16[1024,1152]{1,0:T(8,128)(2,1)} %bitcast.3), custom_call_target="tpu_custom_call" | custom-call | flops 14495514624 | bytes 4194304 | tf_op jit(solution)/shard_map/pallas_call | solution.py:426
  59.4 4.2 %shard_map.69 = (f32[128,8,1152]{2,1,0:T(8,128)}, f32[128,1152]{1,0:T(8,128)}) custom-call(s32[128]{0:T(128)} %counts_ref.1, f32[128,1152]{1,0:T(8,128)} %get-tuple-element.4.pool_hbm, f32[128,1152]{1,0:T(8,128)} %get-tuple-element.5.text_hbm), custom_call_target="tpu_custom_call" | custom-call | bytes 6291456 | tf_op jit(solution)/shard_map/pallas_call | solution.py:465

commit v4 on v3

--- a/solution.py
+++ b/solution.py
@@ -145,7 +145,7 @@
 def kernel(
     log_scale_ref, bias_ref, counts_ref, texts_hbm, clips_hbm,
     pool_ref, text_ref,
-    texts, clips, vids, txts, coef,
+    texts, clips, vids, txts, coef, pool,
     vid_unit, vid_norm, count_col, txt_unit, txt_norm,
     vid_terms, txt_terms, vid_stage, vid_landed, txt_stage, txt_landed, sib_stage, sib_landed,
     load_sems, vid_gather, vid_reduce, txt_gather, txt_reduce, sib_gather, sib_reduce,
@@ -357,11 +357,11 @@
     hand_over(MATE, OWN)
     vid.give(14, 4, 6)
     vid.give(15, 5, 7)
-    txt.give(11, 2)
-    txt.give(13, 3)
     join(MATE)
     txt.give(14, 4, 6)
     txt.give(15, 5, 7)
+    txt.give(11, 2)
+    txt.give(13, 3)
     for i, other in ((18, 10), (16, 12), (19, 11), (17, 13)):
         for side in (vid, txt):
             side.give(i, other)
@@ -369,17 +369,23 @@
     back = scale * vid.own()
     unit = vid_unit[...]
     back = (back - unit * jnp.sum(unit * back, axis=1, keepdims=True)) / vid_norm[...]
-    pool_ref[...] = back / count_col[...]
+    pool[...] = back / count_col[...]
+    pool_out = pltpu.make_async_copy(pool, pool_ref, load_sems.at[2])
+    pool_out.start()
     join(OWN)
     back = scale * txt.own()
     unit = txt_unit[...]
-    text_ref[...] = (back - unit * jnp.sum(unit * back, axis=1, keepdims=True)) / txt_norm[...]
+    txt_unit[...] = (back - unit * jnp.sum(unit * back, axis=1, keepdims=True)) / txt_norm[...]
+    text_out = pltpu.make_async_copy(txt_unit, text_ref, load_sems.at[3])
+    text_out.start()
 
     vid.finish()
     txt.finish()
     for piece in PIECES:
         to_sibling(piece).wait_send()
         terms_to_sibling(piece).wait_send()
+    pool_out.wait()
+    text_out.wait()
 
 
 def spread(counts_ref, pool_hbm, text_hbm, clip_hbm, text_out, pool, text, clip, load_sems, store_sems):
@@ -427,13 +433,14 @@
         kernel,
         out_shape=(own, own),
         in_specs=[smem, smem, vmem, hbm, hbm],
-        out_specs=(vmem, vmem),
+        out_specs=(hbm, hbm),
         scratch_shapes=[
             pltpu.VMEM((ROWS, width), bf16),
             pltpu.VMEM((ROWS * SLOTS, width), bf16),
             pltpu.VMEM((BLOCKS * ROWS, width), bf16),
             pltpu.VMEM((2 * BLOCKS * ROWS, width), bf16),
             pltpu.VMEM((BLOCKS * ROWS, 2 * BLOCKS * ROWS), bf16),
+            pltpu.VMEM((ROWS, width), f32),
             pltpu.VMEM((ROWS, width), f32),
             pltpu.VMEM((ROWS, 1), f32),
             pltpu.VMEM((ROWS, 1), f32),
@@ -447,7 +454,7 @@
             pltpu.VMEM(((BLOCKS - 1) * ROWS, width), bf16),
             pltpu.VMEM((BLOCKS * ROWS, width), bf16),
             pltpu.VMEM((BLOCKS * ROWS, width), bf16),
-            dma((2,)),
+            dma((4,)),
             dma((2, len(GATHER))),
             dma((2, len(REDUCE))),
             dma((2, len(GATHER))),

time: 63.9 us -> 63.6 us (level)
  no operation moved by 1% of the time
where the time goes in v4:
time: 63.6 us; the launch traced here: 63.3 us
  Pallas kernels  61.3 us (96%)
  between operations  2.09 us (3%)
    pallas_call x1, Pallas kernels, on_device(): pl.pallas_call(kernel, out_shape=(own, own), in_specs=[smem, smem, vmem,...  57.1 us
    pallas_call x1, Pallas kernels, on_device(): pl.pallas_call(spread, out_shape=(jax.ShapeDtypeStruct((videos, slots, wi...  4.15 us

profile of v4, /device:TPU:1, one launch (start us, length us, event | category | flops | bytes accessed | tf_op | source)
XLA Modules:
  0.0 63.3 jit_solution(16476761769000521327)
XLA Ops:
  1.9 57.1 %shard_map.68 = (f32[128,1152]{1,0:T(8,128)}, f32[128,1152]{1,0:T(8,128)}) custom-call(f32[1]{0:T(128)S(6)} %copy.7.log_scale_ref, f32[1]{0:T(128)S(6)} %copy.8.bias_ref, s32[1,128]{1,0:T(1,128)} %bitcast.2, bf16[128,1152]{1,0:T(8,128)(2,1)} %texts_hbm.1, bf16[1024,1152]{1,0:T(8,128)(2,1)} %bitcast.3), custom_call_target="tpu_custom_call" | custom-call | flops 14495514624 | bytes 4194304 | tf_op jit(solution)/shard_map/pallas_call | solution.py:432
  59.0 4.2 %shard_map.69 = (f32[128,8,1152]{2,1,0:T(8,128)}, f32[128,1152]{1,0:T(8,128)}) custom-call(s32[128]{0:T(128)} %counts_ref.1, f32[128,1152]{1,0:T(8,128)} %get-tuple-element.4.pool_hbm, f32[128,1152]{1,0:T(8,128)} %get-tuple-element.5.text_hbm), custom_call_target="tpu_custom_call" | custom-call | bytes 6291456 | tf_op jit(solution)/shard_map/pallas_call | solution.py:472

commit v5 on v4

--- a/solution.py
+++ b/solution.py
@@ -61,13 +61,15 @@
     *((0, MATE_FAR, row, 32) for row in (0, 64, 32, 96)),
     *((1, MATE_UP[half], 0, 64) for half in (0, 1)),
     *((2, MATE_DOWN[half], 0, 64) for half in (0, 1)),
-    (1, UP, 0, 64),
-    (2, DOWN, 64, 64),
+    (1, UP, 0, 32),
+    (2, DOWN, 64, 32),
     *((2, FAR, row, 32) for row in (0, 32)),
     *((1, FAR, row, 32) for row in (64, 96)),
     *((0, MATE, row, 64) for row in (0, 64)),
     *((1, UP, row, 32) for row in (64, 96)),
     *((2, DOWN, row, 32) for row in (0, 32)),
+    (1, UP, 32, 32),
+    (2, DOWN, 96, 32),
 )
 PLACE = tuple(sum(message[3] for message in REDUCE[:i]) for i in range(len(REDUCE)))
 
@@ -129,10 +131,12 @@
         self.reduce(i).start()
 
     def own(self):
-        top = self.terms[self.rows(OWN, 0, 64)] + self.arrived(8) + self.arrived(14)
+        top = jnp.concatenate([self.arrived(8), self.arrived(20)], axis=0) + self.arrived(14)
         top = top + jnp.concatenate([self.arrived(18), self.arrived(19)], axis=0)
-        bottom = self.terms[self.rows(OWN, 64, 64)] + self.arrived(9) + self.arrived(15)
+        bottom = jnp.concatenate([self.arrived(9), self.arrived(21)], axis=0) + self.arrived(15)
         bottom = bottom + jnp.concatenate([self.arrived(16), self.arrived(17)], axis=0)
+        top = top + self.terms[self.rows(OWN, 0, 64)]
+        bottom = bottom + self.terms[self.rows(OWN, 64, 64)]
         return jnp.concatenate([top, bottom], axis=0)
 
     def finish(self):
@@ -347,8 +351,8 @@
     join(UP, DOWN, FAR)
     for i, other in ((10, 0), (12, 1), (11, 2), (13, 3)):
         vid.give(i, other)
-    vid.give(8)
-    vid.give(9)
+    for i in (8, 9, 20, 21):
+        vid.give(i)
     txt.give(10, 0)
     txt.give(12, 1)
     txt.give(8)
@@ -362,6 +366,8 @@
     txt.give(15, 5, 7)
     txt.give(11, 2)
     txt.give(13, 3)
+    txt.give(20)
+    txt.give(21)
     for i, other in ((18, 10), (16, 12), (19, 11), (17, 13)):
         for side in (vid, txt):
             side.give(i, other)

time: 63.6 us -> 63.6 us (level)
  no operation moved by 1% of the time
where the time goes in v5:
time: 63.6 us; the launch traced here: 63.4 us
  Pallas kernels  61.4 us (97%)
  between operations  2.09 us (3%)
    pallas_call x1, Pallas kernels, on_device(): pl.pallas_call(kernel, out_shape=(own, own), in_specs=[smem, smem, vmem,...  57.2 us
    pallas_call x1, Pallas kernels, on_device(): pl.pallas_call(spread, out_shape=(jax.ShapeDtypeStruct((videos, slots, wi...  4.15 us

profile of v5, /device:TPU:1, one launch (start us, length us, event | category | flops | bytes accessed | tf_op | source)
XLA Modules:
  0.0 63.4 jit_solution(6776283756926071913)
XLA Ops:
  1.9 57.2 %shard_map.68 = (f32[128,1152]{1,0:T(8,128)}, f32[128,1152]{1,0:T(8,128)}) custom-call(f32[1]{0:T(128)S(6)} %copy.7.log_scale_ref, f32[1]{0:T(128)S(6)} %copy.8.bias_ref, s32[1,128]{1,0:T(1,128)} %bitcast.2, bf16[128,1152]{1,0:T(8,128)(2,1)} %texts_hbm.1, bf16[1024,1152]{1,0:T(8,128)(2,1)} %bitcast.3), custom_call_target="tpu_custom_call" | custom-call | flops 14495514624 | bytes 4194304 | tf_op jit(solution)/shard_map/pallas_call | solution.py:438
  59.1 4.2 %shard_map.69 = (f32[128,8,1152]{2,1,0:T(8,128)}, f32[128,1152]{1,0:T(8,128)}) custom-call(s32[128]{0:T(128)} %counts_ref.1, f32[128,1152]{1,0:T(8,128)} %get-tuple-element.4.pool_hbm, f32[128,1152]{1,0:T(8,128)} %get-tuple-element.5.text_hbm), custom_call_target="tpu_custom_call" | custom-call | bytes 6291456 | tf_op jit(solution)/shard_map/pallas_call | solution.py:478
